TPU v7x, 32 devices: a whole 2x2x4 slice. The times are simulated.
32 devices in a mesh: tm: 4 (over y, x), dp: 8 (over z, core).
Axes of the slice: x: 2, y: 2, z: 4, core: 2. Of those that a mesh axis runs over, the one named last changes fastest.
Arguments:
- features: bfloat16 [8, 8, 16, 24, 384], P('dp', 'tm'), may hold values from -60 to 60
- conv_weight: bfloat16 [10368, 384], replicated, may hold values from -0.0625 to 0.0625
- up_weight: bfloat16 [1152, 768], replicated, may hold values from -0.1875 to 0.1875
- cotangent: bfloat16 [8, 16, 16, 24, 384], P('dp', 'tm'), may hold values from -6 to 6
Outputs:
- features_grad: bfloat16 [8, 8, 16, 24, 384], P('dp', 'tm')
- grad_conv: float32 [10368, 384], P('dp', 'tm')
- grad_up: float32 [1152, 768], P('dp', 'tm')
All inputs are finite; a program needn't handle non-finite values.
Results may differ from a plain program's by a relative error of at most 0.0049.
Values may be sent and summed in bfloat16 or wider, within the bound.
A program may use at most 128 MiB of HBM per device.

v0:
```python
import math

import jax
import jax.numpy as jnp
from jax import lax
from jax.sharding import PartitionSpec as P

G = 32


EPSILON = 1e-06


def from_behind(value, axis, steps):
    count = lax.axis_size(axis)
    first, last = (max(0, -steps), min(count, count - steps))
    return lax.ppermute(value, axis, [(source, source + steps) for source in range(first, last)])


def norm_act(field):
    shape = field.shape
    grouped = field.reshape(shape[:-3] + (shape[-3] * shape[-2], G, shape[-1] // G))
    center = grouped - jnp.mean(grouped, axis=(-3, -1), keepdims=True)
    spread = jnp.mean(center * center, axis=(-3, -1), keepdims=True)
    normed = center * lax.rsqrt(spread + EPSILON)
    return jax.nn.silu(normed).reshape(shape)


def space_pad(field):
    return jnp.pad(field, ((0, 0), (0, 0), (1, 1), (1, 1), (0, 0)))


def stack_taps(padded, frames, height, breadth):
    pieces = [
        padded[
            :,
            time_tap : time_tap + frames,
            high_tap : high_tap + height,
            wide_tap : wide_tap + breadth,
            :,
        ]
        for time_tap in range(3)
        for high_tap in range(3)
        for wide_tap in range(3)
    ]
    joined = jnp.concatenate(pieces, axis=-1)
    return joined.reshape(-1, joined.shape[-1])


def stack_times(padded, frames):
    pieces = [padded[:, time_tap : time_tap + frames] for time_tap in range(3)]
    joined = jnp.concatenate(pieces, axis=-1)
    return joined.reshape(-1, joined.shape[-1])


def contract_rows(left, right):
    return lax.dot_general(
        left, right, (((0,), (0,)), ((), ())), preferred_element_type=jnp.float32
    )


def shards(features, conv_weight, up_weight, cotangent):
    crop_count, frames, height, breadth, channels = features.shape
    block_shape = features.shape
    feature_field = features.astype(jnp.float32)
    act_float, pullback = jax.vjp(norm_act, feature_field)
    act = act_float.astype(jnp.bfloat16)
    act_prior = from_behind(act, "tm", 1)
    act_cols = stack_taps(
        space_pad(jnp.concatenate([act_prior, act], axis=1)), frames, height, breadth
    )
    conv_out = jnp.dot(act_cols, conv_weight, preferred_element_type=jnp.float32)
    hidden = (
        (feature_field.reshape(-1, channels) + conv_out).astype(jnp.bfloat16).reshape(block_shape)
    )
    hidden_prior = from_behind(hidden, "tm", 1)
    hidden_cols = stack_times(jnp.concatenate([hidden_prior, hidden], axis=1), frames)
    up_grad = cotangent.reshape(crop_count, frames, 2, height, breadth, channels)
    up_grad = up_grad.transpose(0, 1, 3, 4, 2, 5).reshape(
        crop_count, frames, height, breadth, 2 * channels
    )
    up_next = from_behind(up_grad, "tm", -1)
    up_cols = stack_times(jnp.concatenate([up_grad, up_next], axis=1), frames)
    up_flip = (
        up_weight.reshape(3, channels, 2 * channels)[::-1]
        .transpose(0, 2, 1)
        .reshape(6 * channels, channels)
    )
    hidden_grad = jnp.dot(up_cols, up_flip, preferred_element_type=jnp.float32)
    conv_grad = hidden_grad.astype(jnp.bfloat16)
    up_flat = up_grad.reshape(-1, 2 * channels)
    conv_field = conv_grad.reshape(block_shape)
    conv_next = from_behind(conv_field, "tm", -1)
    conv_cols = stack_taps(
        space_pad(jnp.concatenate([conv_field, conv_next], axis=1)), frames, height, breadth
    )
    conv_flip = (
        conv_weight.reshape(3, 3, 3, channels, channels)[::-1, ::-1, ::-1]
        .transpose(0, 1, 2, 4, 3)
        .reshape(27 * channels, channels)
    )
    act_grad = jnp.dot(conv_cols, conv_flip, preferred_element_type=jnp.float32)
    (norm_grad,) = pullback(act_grad.reshape(block_shape))
    features_grad = (hidden_grad.reshape(block_shape) + norm_grad).astype(jnp.bfloat16)
    data_count = lax.axis_size("dp")
    time_count = lax.axis_size("tm")
    scale = 1.0 / math.sqrt(crop_count * frames * height * breadth * data_count * time_count)
    up_part = lax.psum_scatter(
        contract_rows(hidden_cols, up_flat), "dp", scatter_dimension=0, tiled=True
    )
    grad_up = lax.psum_scatter(up_part, "tm", scatter_dimension=1, tiled=True) * scale
    conv_part = lax.psum_scatter(
        contract_rows(act_cols, conv_grad), "dp", scatter_dimension=0, tiled=True
    )
    grad_conv = lax.psum_scatter(conv_part, "tm", scatter_dimension=1, tiled=True) * scale
    return (features_grad, grad_conv, grad_up)


def solution(mesh):
    in_specs = (P("dp", "tm", None, None, None), P(), P(), P("dp", "tm", None, None, None))
    out_specs = (P("dp", "tm", None, None, None), P("dp", "tm"), P("dp", "tm"))
    return jax.shard_map(shards, mesh=mesh, in_specs=in_specs, out_specs=out_specs, check_vma=False)
```

profile of v0, /device:TPU:0, one launch (start us, length us, event | category | flops | bytes accessed | tf_op | source)
XLA Modules:
  0.0 464.4 jit_solution(9162958915427405360)
XLA Ops:
  7.2 2.5 copy.68
  15.6 7.6 %reverse_bitcast_fusion = bf16[3,3,3,384,384]{3,4,2,1,0:T(8,128)(2,1)} fusion(bf16[3,3,3,384,384]{4,3,2,1,0:T(8,128)(2,1)} %bitcast.73), kind=kLoop, calls=%fused_computation | loop fusion | bytes 15925248 | tf_op jit(solution)/shard_map/transpose | solution.py:99
  23.2 15.1 %copy.47 = bf16[3,3,3,384,384]{4,3,2,1,0:T(8,128)(2,1)} copy(bf16[3,3,3,384,384]{3,4,2,1,0:T(8,128)(2,1)} %reverse_bitcast_fusion) | data formatting | bytes 15925248 | tf_op jit(solution)/shard_map/transpose | solution.py:99
  38.4 5.0 %copy.49 = f32[1,2,16,24,384]{3,2,1,4,0:T(8,128)} copy(bf16[1,2,16,24,384]{4,3,2,1,0:T(8,128)(2,1)S(1)} %copy-done) | data formatting | bytes 1769472 | tf_op jit(solution)/shard_map/convert_element_type | solution.py:65
  45.7 4.3 fusion.53
  52.7 5.9 %reshape.274 = f32[1,2,384,32,12]{2,1,4,3,0:T(2,128)S(1)} reshape(f32[1,2,16,24,384]{3,2,1,4,0:T(8,128)} %copy.49) | data formatting | bytes 2359296 | tf_op jit(solution)/shard_map/jvp()/reshape | solution.py:22
  58.7 10.1 %collective-permute-done.1 = bf16[1,2,16,24,384]{4,3,2,1,0:T(8,128)(2,1)S(1)} collective-permute-done((bf16[1,2,16,24,384]{4,3,2,1,0:T(8,128)(2,1)S(1)}, bf16[1,2,16,24,384]{4,3,2,1,0:T(8,128)(2,1)S(1)}, u32[]{:S(2)}, u32[]{:S(2)}) %collective-permute-start.1) | collective-permute-done | bytes 589856 | tf_op jit(solution)/shard_map/ppermute | solution.py:17
  68.9 3.3 pad_slice_fusion.24
  98.4 11.4 %fusion.54 = f32[768,384]{1,0:T(8,128)S(1)} fusion(bf16[768,10368]{1,0:T(8,128)(2,1)} %constant_dynamic-update-slice_fusion, bf16[10368,384]{1,0:T(8,128)(2,1)S(1)} %bitcast.78), kind=kOutput, calls=%fused_computation.159 | convolution fusion | flops 6115295232 | bytes 25067520 | tf_op jit(solution)/shard_map/dot_general | solution.py:102
  111.1 2.9 reshape_reshape.7
  120.0 2.9 multiply_convert_fusion
  123.0 4.6 collective-permute-start.2
  127.6 11.6 %collective-permute-done.2 = bf16[1,2,16,24,384]{4,3,2,1,0:T(8,128)(2,1)S(1)} collective-permute-done((bf16[1,2,16,24,384]{4,3,2,1,0:T(8,128)(2,1)S(1)}, bf16[1,2,16,24,384]{4,3,2,1,0:T(8,128)(2,1)S(1)}, u32[]{:S(2)}, u32[]{:S(2)}) %collective-permute-start.2) | collective-permute-done | bytes 589856 | tf_op jit(solution)/shard_map/ppermute | solution.py:17
  144.3 6.0 %copy-done.5 = bf16[1,2,16,24,10368]{4,3,2,1,0:T(8,128)(2,1)} copy-done((bf16[1,2,16,24,10368]{4,3,2,1,0:T(8,128)(2,1)}, bf16[1,2,16,24,10368]{4,3,2,1,0:T(8,128)(2,1)S(1)}, u32[]{:S(2)}) %copy-start.5) | copy-done | bytes 15925272
  150.3 11.8 %fusion.12 = bf16[768,384]{1,0:T(8,128)(2,1)S(1)} fusion(f32[768,384]{1,0:T(8,128)S(1)} %bitcast.116, bf16[768,10368]{1,0:T(8,128)(2,1)} %bitcast.123, bf16[10368,384]{1,0:T(8,128)(2,1)S(1)} %bitcast.75), kind=kOutput, calls=%fused_computation.73 | convolution fusion | flops 6115885056 | bytes 25657344 | tf_op jit(solution)/shard_map/dot_general | solution.py:72
  162.2 4.8 %collective-permute-start.3 = (bf16[1,2,16,24,384]{4,3,2,1,0:T(8,128)(2,1)S(1)}, bf16[1,2,16,24,384]{4,3,2,1,0:T(8,128)(2,1)S(1)}, u32[]{:S(2)}, u32[]{:S(2)}) collective-permute-start(bf16[1,2,16,24,384]{4,3,2,1,0:T(8,128)(2,1)S(1)} %bitcast.117), channel_id=1, source_target_pairs={{0,8},{8,16},{16,24},{1,9},{9,17},{17,25},{2,10},{10,18},{18,26},{... | collective-permute-start | bytes 1769480 | tf_op jit(solution)/shard_map/ppermute | solution.py:17
  167.0 10.5 %collective-permute-done.3 = bf16[1,2,16,24,384]{4,3,2,1,0:T(8,128)(2,1)S(1)} collective-permute-done((bf16[1,2,16,24,384]{4,3,2,1,0:T(8,128)(2,1)S(1)}, bf16[1,2,16,24,384]{4,3,2,1,0:T(8,128)(2,1)S(1)}, u32[]{:S(2)}, u32[]{:S(2)}) %collective-permute-start.3) | collective-permute-done | bytes 589856 | tf_op jit(solution)/shard_map/ppermute | solution.py:17
  177.6 3.4 fusion.6
  181.0 15.2 %fusion.55 = f32[10368,384]{1,0:T(8,128)} fusion(bf16[768,10368]{1,0:T(8,128)(2,1)} %bitcast.124, bf16[768,384]{1,0:T(8,128)(2,1)S(1)} %get-tuple-element.49), kind=kOutput, calls=%fused_computation.160 | convolution fusion | flops 6115295232 | bytes 32440320 | tf_op jit(solution)/shard_map/dot_general | solution.py:57
  196.3 31.4 %reduce-scatter.11.cloned.1.call-done = f32[144,768]{1,0:T(8,128)} async-done(((f32[1152,768]{1,0:T(8,128)}), f32[144,768]{1,0:T(8,128)}) %reduce-scatter.11.cloned.1.call-update) | async-done | bytes 442384 | tf_op jit(solution)/shard_map/reduce_scatter | solution.py:108
  230.0 159.5 %reduce-scatter.9.cloned.1.call-done = f32[1296,384]{1,0:T(8,128)} async-done(((f32[10368,384]{1,0:T(8,128)}), f32[1296,384]{1,0:T(8,128)}) %reduce-scatter.9.cloned.1.call-update) | async-done | bytes 1990672 | tf_op jit(solution)/shard_map/reduce_scatter | solution.py:112
  389.4 3.0 copy.56
  392.5 24.4 %reduce-scatter.15.cloned.1.call-done = f32[192,144]{1,0:T(8,128)} async-done(((f32[768,144]{1,0:T(8,128)}), f32[192,144]{1,0:T(8,128)}) %reduce-scatter.15.cloned.1.call-update) | async-done | bytes 110608
  418.5 36.9 %reduce-scatter.13.cloned.1.call-done = f32[96,1296]{1,0:T(8,128)} async-done(((f32[384,1296]{1,0:T(8,128)}), f32[96,1296]{1,0:T(8,128)}) %reduce-scatter.13.cloned.1.call-update) | async-done | bytes 497680
  (130 shorter events, 56.2 us)
Async XLA Ops:
  7.2 220.5 %reduce-scatter.11.cloned.1.call-start = ((), (), s32[]{:S(2)}) async-start(), calls=%async_computation.5 | async-start | bytes 3981312 | tf_op jit(solution)/shard_map/reduce_scatter | solution.py:108
  10.5 2.7 copy-start.1
  10.5 33.2 %collective-permute-start = (bf16[1,2,16,24,768]{4,3,2,1,0:T(8,128)(2,1)S(1)}, bf16[1,2,16,24,768]{4,3,2,1,0:T(8,128)(2,1)}, u32[]{:S(2)}, u32[]{:S(2)}) collective-permute-start(bf16[1,2,16,24,768]{4,3,2,1,0:T(8,128)(2,1)S(1)} %reshape.267), channel_id=1, source_target_pairs={{8,0},{16,8},{24,16},{9,1},{17,9},{25,17},{10,2},{18,10},{26,18},{... | collective-permute-start | bytes 3538952 | tf_op jit(solution)/shard_map/ppermute | solution.py:17
  23.2 15.1 %copy-start = (bf16[1,2,16,24,384]{4,3,2,1,0:T(8,128)(2,1)S(1)}, bf16[1,2,16,24,384]{4,3,2,1,0:T(8,128)(2,1)}, u32[]{:S(2)}) copy-start(bf16[1,2,16,24,384]{4,3,2,1,0:T(8,128)(2,1)} %param.4) | copy-start | bytes 1769476
  43.7 1.7 copy-start.2
  43.7 2.0 copy-start.3
  50.0 18.8 %collective-permute-start.1 = (bf16[1,2,16,24,384]{4,3,2,1,0:T(8,128)(2,1)S(1)}, bf16[1,2,16,24,384]{4,3,2,1,0:T(8,128)(2,1)S(1)}, u32[]{:S(2)}, u32[]{:S(2)}) collective-permute-start(bf16[1,2,16,24,384]{4,3,2,1,0:T(8,128)(2,1)S(1)} %bitcast.79), channel_id=1, source_target_pairs={{8,0},{16,8},{24,16},{9,1},{17,9},{25,17},{10,2},{18,10},{26,18},{... | collective-permute-start | bytes 1769480 | tf_op jit(solution)/shard_map/ppermute | solution.py:17
  52.0 6.7 %copy-start.7 = (f32[2,32]{1,0:T(2,128)}, f32[2,32]{1,0:T(2,128)S(1)}, u32[]{:S(2)}) copy-start(f32[2,32]{1,0:T(2,128)S(1)} %reduce_sum.70) | copy-start | bytes 772
  52.0 0.5 copy-start.6
  86.1 12.3 %slice-start.2 = ((s8[7962624]{0:T(1024)(128)(4,1)}), s8[4194304]{0:T(1024)(128)(4,1)S(1)}, s32[]{:S(2)}) async-start(s8[7962624]{0:T(1024)(128)(4,1)} %bitcast.76), calls=%async_computation.10 | async-start | bytes 8388608
  91.7 6.8 %slice-start.3 = ((s8[7962624]{0:T(1024)(128)(4,1)}), s8[3768320]{0:T(1024)(128)(4,1)S(1)}, s32[]{:S(2)}) async-start(s8[7962624]{0:T(1024)(128)(4,1)} %bitcast.76), calls=%async_computation.11 | async-start | bytes 7536640
  123.0 16.2 %collective-permute-start.2 = (bf16[1,2,16,24,384]{4,3,2,1,0:T(8,128)(2,1)S(1)}, bf16[1,2,16,24,384]{4,3,2,1,0:T(8,128)(2,1)S(1)}, u32[]{:S(2)}, u32[]{:S(2)}) collective-permute-start(bf16[1,2,16,24,384]{4,3,2,1,0:T(8,128)(2,1)S(1)} %get-tuple-element.47), channel_id=1, source_target_pairs={{0,8},{8,16},{16,24},{1,9},{9,17},{17,25},{2,10},{10,18},{18,26},{... | collective-permute-start | bytes 1769480 | tf_op jit(solution)/shard_map/ppermute | solution.py:17
  142.6 7.7 %slice-start = ((s8[7962624]{0:T(1024)(128)(4,1)}), s8[4194304]{0:T(1024)(128)(4,1)S(1)}, s32[]{:S(2)}) async-start(s8[7962624]{0:T(1024)(128)(4,1)} %bitcast.74), calls=%async_computation.8 | async-start | bytes 8388608
  143.4 6.9 %slice-start.1 = ((s8[7962624]{0:T(1024)(128)(4,1)}), s8[3768320]{0:T(1024)(128)(4,1)S(1)}, s32[]{:S(2)}) async-start(s8[7962624]{0:T(1024)(128)(4,1)} %bitcast.74), calls=%async_computation.9 | async-start | bytes 7536640
  144.3 6.0 %copy-start.5 = (bf16[1,2,16,24,10368]{4,3,2,1,0:T(8,128)(2,1)}, bf16[1,2,16,24,10368]{4,3,2,1,0:T(8,128)(2,1)S(1)}, u32[]{:S(2)}) copy-start(bf16[1,2,16,24,10368]{4,3,2,1,0:T(8,128)(2,1)S(1)} %fusion.48) | copy-start | bytes 47775748
  162.2 15.4 %copy-start.4 = (bf16[96,8,2,384]{3,1,2,0:T(8,128)(2,1)S(1)}, bf16[96,8,2,384]{3,1,2,0:T(8,128)(2,1)}, u32[]{:S(2)}) copy-start(bf16[96,8,2,384]{3,1,2,0:T(8,128)(2,1)} %copy.61) | copy-start | bytes 3538948
  162.2 15.3 %collective-permute-start.3 = (bf16[1,2,16,24,384]{4,3,2,1,0:T(8,128)(2,1)S(1)}, bf16[1,2,16,24,384]{4,3,2,1,0:T(8,128)(2,1)S(1)}, u32[]{:S(2)}, u32[]{:S(2)}) collective-permute-start(bf16[1,2,16,24,384]{4,3,2,1,0:T(8,128)(2,1)S(1)} %bitcast.117), channel_id=1, source_target_pairs={{0,8},{8,16},{16,24},{1,9},{9,17},{17,25},{2,10},{10,18},{18,26},{... | collective-permute-start | bytes 1769480 | tf_op jit(solution)/shard_map/ppermute | solution.py:17
  181.0 208.5 %reduce-scatter.9.cloned.1.call-start = ((), (), s32[]{:S(2)}) async-start(), calls=%async_computation.4 | async-start | bytes 17915904 | tf_op jit(solution)/shard_map/reduce_scatter | solution.py:112
  196.3 220.5 %reduce-scatter.15.cloned.1.call-start = ((), (), s32[]{:S(2)}) async-start(), calls=%async_computation.7 | async-start | bytes 983040
  229.9 225.5 %reduce-scatter.13.cloned.1.call-start = ((), (), s32[]{:S(2)}) async-start(), calls=%async_computation.6 | async-start | bytes 2703360
Sparse Core Ops, SparseCore 0:
  181.1 46.5 reduce-scatter.10
  230.2 159.2 reduce-scatter.8
  392.3 24.4 reduce-scatter.14
  419.7 35.7 reduce-scatter.12
where the time goes:
time: 465 us; the launch traced here: 464 us
  waiting for transfers between devices  284 us (61%)
  local copies, waits for them, and re-layouts  96.5 us (21%)
  matrix products  46.1 us (10%)
  between operations  14.2 us (3%)
  starting transfers between devices  12.4 us (3%)
  other arithmetic  10.9 us (2%)
    reduce_scatter x1, waiting for transfers between devices, shards(): lax.psum_scatter(contract_rows(act_cols, conv_grad), 'dp', scatter_dimens...  159 us
    unnamed x6, waiting for transfers between devices  61.3 us
    unnamed x81, local copies, waits for them, and re-layouts  45.9 us
    ppermute x4, waiting for transfers between devices, from_behind(): lax.ppermute(value, axis, [(source, source + steps) for source in range(f...  32.1 us
    reduce_scatter x1, waiting for transfers between devices, shards(): lax.psum_scatter(contract_rows(hidden_cols, up_flat), 'dp', scatter_dimen...  31.4 us
    transpose x2, local copies, waits for them, and re-layouts, shards(): conv_flip = conv_weight.reshape(3, 3, 3, channels, channels)[::-1, ::-1,...  22.7 us
    dot_general x2, matrix products, contract_rows(): lax.dot_general(left, right, (((0,), (0,)), ((), ())), preferred_element_...  18.6 us
    ppermute x4, starting transfers between devices, from_behind(): lax.ppermute(value, axis, [(source, source + steps) for source in range(f...  12.3 us
  transfers between devices with their start and end apart: 8, of which 7 were waited for; matrix products, arithmetic and copies ran while one was open for 13% of the time, Pallas kernels for 0%

commit v1 on v0

v1 whole, which is shorter than its diff:
```python
import functools
import math

import jax
import jax.numpy as jnp
from jax import lax
from jax.experimental import pallas as pl
from jax.experimental.pallas import tpu as pltpu
from jax.sharding import PartitionSpec as P

G = 32


EPSILON = 1e-06
LANES = 128


def from_behind(value, axis, steps):
    count = lax.axis_size(axis)
    first, last = (max(0, -steps), min(count, count - steps))
    return lax.ppermute(value, axis, [(source, source + steps) for source in range(first, last)])


def exchange(blocks, axis, kind):
    count = lax.axis_size(axis)
    me = lax.axis_index(axis)
    total = lax.dynamic_index_in_dim(blocks, me, 0, keepdims=False)
    for step in range(1, count):
        pairs = [(place, place ^ step) for place in range(count)]
        sent = lax.dynamic_index_in_dim(blocks, me ^ step, 0, keepdims=False).astype(kind)
        total = total + lax.ppermute(sent, axis, pairs).astype(jnp.float32)
    return total


def reduce_data(part):
    count = lax.axis_size("dp")
    me = lax.axis_index("dp")
    rows = part.shape[0] // count
    blocks = part.reshape((count // 2, 2, rows) + part.shape[1:])
    core = me % 2
    kept = lax.dynamic_index_in_dim(blocks, core, 1, keepdims=False)
    sent = lax.dynamic_index_in_dim(blocks, 1 - core, 1, keepdims=False)
    pair = kept + lax.ppermute(sent, "dp", [(place, place ^ 1) for place in range(count)])
    home = me // 2
    total = lax.dynamic_index_in_dim(pair, home, 0, keepdims=False)
    for step in range(1, count // 2):
        pairs = [(place, place ^ (2 * step)) for place in range(count)]
        piece = lax.dynamic_index_in_dim(pair, home ^ step, 0, keepdims=False)
        piece = lax.ppermute(piece.astype(jnp.bfloat16), "dp", pairs)
        total = total + piece.astype(jnp.float32)
    return total


def group_mean(field):
    crops, frames, height, breadth, channels = field.shape
    sums = jnp.sum(field, axis=(2, 3)).reshape(crops, frames, G, channels // G)
    means = jnp.sum(sums, axis=-1, keepdims=True) / (height * breadth * channels // G)
    spread = jnp.broadcast_to(means, sums.shape).reshape(crops, frames, channels)
    return spread[:, :, None, None, :]


def weight_body(frames, breadth, left_ref, right_ref, out_ref):
    high = 2 - pl.program_id(0) // 3
    wide = 2 - lax.rem(pl.program_id(0), 3)
    height, lanes = right_ref.shape[-2:]
    windows = [
        right_ref[high, 2 - tap : 2 - tap + frames, pl.ds(wide, breadth)].reshape(
            frames * breadth * height, lanes
        )
        for tap in range(3)
    ]
    product = jnp.dot(
        left_ref[...], jnp.concatenate(windows, axis=1), preferred_element_type=jnp.float32
    )
    for tap in range(3):
        out_ref[tap, 0] = product[:, tap * lanes : tap * lanes + out_ref.shape[-1]]


def weight_gradient(act_all, columns):
    frames, height, breadth, channels = act_all.shape
    width = columns.shape[-1]
    lanes = -(-width // LANES) * LANES
    left = act_all.transpose(3, 0, 2, 1).reshape(channels, -1)
    turned = jnp.pad(
        columns.transpose(0, 2, 1, 3), ((0, 2), (1, 1), (1, 1), (0, lanes - width))
    )
    right = jnp.stack([turned[:, :, high : high + height] for high in range(3)])
    positions = frames * height * breadth
    out = pl.pallas_call(
        functools.partial(weight_body, frames, breadth),
        grid=(9,),
        in_specs=[
            pl.BlockSpec(left.shape, lambda step: (0, 0)),
            pl.BlockSpec(right.shape, lambda step: (0, 0, 0, 0, 0)),
        ],
        out_specs=pl.BlockSpec((3, 1, channels, width), lambda step: (0, step, 0, 0)),
        out_shape=jax.ShapeDtypeStruct((3, 9, channels, width), jnp.float32),
        compiler_params=pltpu.CompilerParams(vmem_limit_bytes=48 * 1024 * 1024),
        cost_estimate=pl.CostEstimate(
            flops=54 * positions * channels * lanes,
            bytes_accessed=2 * (left.size + right.size) + 4 * 27 * channels * width,
            transcendentals=0,
        ),
    )(left, right)
    return out.reshape(27 * channels, width)


def shards(features, conv_weight, up_weight, cotangent):
    crop_count, frames, height, breadth, channels = features.shape
    data_count = lax.axis_size("dp")
    time_count = lax.axis_size("tm")
    scale = 1.0 / math.sqrt(crop_count * frames * height * breadth * data_count * time_count)
    kernel = conv_weight.reshape(3, 3, 3, channels, channels)
    me = lax.axis_index("tm")

    up_grad = jnp.concatenate([cotangent[:, 0::2], cotangent[:, 1::2]], axis=-1)
    taps = lax.dot_general(
        up_grad.reshape(-1, 2 * channels),
        up_weight,
        (((1,), (1,)), ((), ())),
        preferred_element_type=jnp.float32,
    ).reshape((crop_count, frames, height, breadth, 3 * channels))

    def share(frame):
        terms = [
            taps[:, frame + 2 - k, :, :, k * channels : (k + 1) * channels]
            for k in range(3)
            if 0 <= frame + 2 - k < frames
        ]
        return functools.reduce(jnp.add, terms)

    far = jnp.stack([share(-2), share(-1)], axis=1)
    before = from_behind(far.astype(jnp.bfloat16), "tm", -1)

    field = features.astype(jnp.float32)
    center = field - group_mean(field)
    inverse = lax.rsqrt(group_mean(center * center) + EPSILON)
    normed = center * inverse
    gate = 1.0 / (1.0 + jnp.exp(-normed))
    act = (normed * gate).astype(jnp.bfloat16)
    act_prior = from_behind(act[:, frames - 2 :], "tm", 1)

    hidden_grad = jnp.stack([share(frame) for frame in range(frames)], axis=1)
    hidden_grad = hidden_grad.at[:, frames - 2 :].add(before.astype(jnp.float32))
    conv_grad = hidden_grad.astype(jnp.bfloat16)
    conv_next = from_behind(conv_grad[:, :2], "tm", -1)

    width = channels // time_count
    gathered = (crop_count, time_count) + features.shape[1:]
    act_sent, _ = lax.optimization_barrier((act, before))
    act_all = lax.dynamic_update_slice(
        jnp.zeros(gathered, jnp.bfloat16), act[:, None], (0, me, 0, 0, 0, 0)
    )
    own = lax.dynamic_slice_in_dim(conv_grad, me * width, width, 4)
    conv_columns = lax.dynamic_update_slice(
        jnp.zeros(gathered[:-1] + (width,), jnp.bfloat16), own[:, None], (0, me, 0, 0, 0, 0)
    )
    for step in range(1, time_count):
        pairs = [(place, place ^ step) for place in range(time_count)]
        other = me ^ step
        piece = lax.dynamic_slice_in_dim(conv_grad, other * width, width, 4)
        piece = lax.ppermute(piece, "tm", pairs)
        conv_columns = lax.dynamic_update_slice(
            conv_columns, piece[:, None], (0, other, 0, 0, 0, 0)
        )
        block = lax.ppermute(act_sent, "tm", pairs)
        act_all = lax.dynamic_update_slice(act_all, block[:, None], (0, other, 0, 0, 0, 0))
    whole = (crop_count, time_count * frames, height, breadth)
    act_all = act_all.reshape(whole + (channels,))
    conv_columns = conv_columns.reshape(whole + (width,))

    conv_part = weight_gradient(act_all[0], conv_columns[0])
    for crop in range(1, crop_count):
        conv_part = conv_part + weight_gradient(act_all[crop], conv_columns[crop])

    conv_out = lax.conv_general_dilated(
        jnp.concatenate([act_prior, act], axis=1),
        kernel,
        (1, 1, 1),
        ((0, 0), (1, 1), (1, 1)),
        dimension_numbers=("NDHWC", "DHWIO", "NDHWC"),
        preferred_element_type=jnp.float32,
    )
    hidden = (field + conv_out).astype(jnp.bfloat16)
    hidden_prior = from_behind(hidden[:, frames - 2 :], "tm", 1)
    hidden_ext = jnp.concatenate([hidden_prior, hidden], axis=1)
    hidden_cols = jnp.concatenate([hidden_ext[:, k : k + frames] for k in range(3)], axis=-1)
    hidden_cols = hidden_cols.reshape(-1, 3 * channels)
    halves = [
        lax.dot_general(
            hidden_cols,
            cotangent[:, half::2].reshape(-1, channels),
            (((0,), (0,)), ((), ())),
            preferred_element_type=jnp.float32,
        )
        for half in range(2)
    ]
    conv_ext = jnp.concatenate([conv_grad, conv_next], axis=1)
    conv_ext, conv_part, up_part = lax.optimization_barrier(
        (conv_ext, conv_part, jnp.concatenate(halves, axis=1))
    )
    grad_conv = reduce_data(conv_part) * scale
    up_part = reduce_data(up_part)
    up_width = 2 * channels // time_count
    up_part = up_part.reshape(-1, time_count, up_width).transpose(1, 0, 2)
    grad_up = exchange(up_part, "tm", jnp.float32) * scale

    act_grad = lax.conv_general_dilated(
        conv_ext,
        lax.rev(kernel, (0, 1, 2)),
        (1, 1, 1),
        ((0, 0), (1, 1), (1, 1)),
        dimension_numbers=("NDHWC", "DHWOI", "NDHWC"),
        preferred_element_type=jnp.float32,
    )
    normed_grad = act_grad * gate * (1.0 + normed * (1.0 - gate))
    first = group_mean(normed_grad)
    second = group_mean(normed_grad * normed)
    norm_grad = inverse * (normed_grad - first - normed * second)
    features_grad = (hidden_grad + norm_grad).astype(jnp.bfloat16)
    return (features_grad, grad_conv, grad_up)


def solution(mesh):
    in_specs = (P("dp", "tm", None, None, None), P(), P(), P("dp", "tm", None, None, None))
    out_specs = (P("dp", "tm", None, None, None), P("dp", "tm"), P("dp", "tm"))
    return jax.shard_map(shards, mesh=mesh, in_specs=in_specs, out_specs=out_specs, check_vma=False)
```

time: 465 us -> 225 us (0.48)
  waiting for transfers between devices: 284 us -> 60.5 us
  local copies, waits for them, and re-layouts: 96.5 us -> 53.3 us
  starting transfers between devices: 12.4 us -> 35.9 us
  Pallas kernels: 0 us -> 13.6 us
  between operations: 14.2 us -> 1.19 us
  other arithmetic: 10.9 us -> 20.6 us
  matrix products: 46.1 us -> 39.1 us
    reduce_scatter x2 -> x0, waiting for transfers between devices: 191 us -> none  [the longest x1 159 us: shards(): lax.psum_scatter(contract_rows(act_cols, conv_grad), 'dp', scatter_dimens...]
    unnamed x6 -> x0, waiting for transfers between devices: 61.3 us -> none
    ppermute x0 -> x17, waiting for transfers between devices: none -> 52.6 us  [the longest x6 28 us: reduce_data(): piece = lax.ppermute(piece.astype(jnp.bfloat16), 'dp', pairs)]
    dot_general x5 -> x3, matrix products: 46.1 us -> 6.8 us  [the longest x2 5.05 us: shards(): lax.dot_general(hidden_cols, cotangent[:, half::2].reshape(-1, channels),...]
    unnamed x81 -> x41, local copies, waits for them, and re-layouts: 45.9 us -> 7.99 us
    conv_general_dilated x0 -> x2, matrix products: none -> 32.3 us  [the longest x1 18.7 us: shards(): lax.conv_general_dilated(jnp.concatenate([act_prior, act], axis=1), kerne...]
    transpose x4 -> x0, local copies, waits for them, and re-layouts: 25.1 us -> none  [the longest x2 22.7 us: shards(): conv_flip = conv_weight.reshape(3, 3, 3, channels, channels)[::-1, ::-1,...]
    ppermute x4, waiting for transfers between devices: 32.1 us -> 7.88 us  [from_behind(): lax.ppermute(value, axis, [(source, source + steps) for source in range(f...]
  transfers between devices with their start and end apart: 8 -> 21, of which waited for: 7 -> 9; matrix products, arithmetic and copies ran while one was open for 13% -> 42% of each run, Pallas kernels for 0% -> 6%
where the time goes in v1:
time: 225 us; the launch traced here: 224 us
  waiting for transfers between devices  60.5 us (27%)
  local copies, waits for them, and re-layouts  53.3 us (24%)
  matrix products  39.1 us (17%)
  starting transfers between devices  35.9 us (16%)
  other arithmetic  20.6 us (9%)
  Pallas kernels  13.6 us (6%)
    ppermute x6, waiting for transfers between devices, reduce_data(): piece = lax.ppermute(piece.astype(jnp.bfloat16), 'dp', pairs)  28 us
    ppermute x3, waiting for transfers between devices, shards(): piece = lax.ppermute(piece, 'tm', pairs)  22.7 us
    conv_general_dilated x1, matrix products, shards(): lax.conv_general_dilated(jnp.concatenate([act_prior, act], axis=1), kerne...  18.7 us
    conv_general_dilated x1, matrix products, shards(): lax.conv_general_dilated(conv_ext, lax.rev(kernel, (0, 1, 2)), (1, 1, 1),...  13.6 us
    pallas_call x1, Pallas kernels, weight_gradient(): pl.pallas_call(functools.partial(weight_body, frames, breadth), grid=(9,)...  13.6 us
    ppermute x4, starting transfers between devices, from_behind(): lax.ppermute(value, axis, [(source, source + steps) for source in range(f...  12.2 us
    dynamic_update_slice x4, local copies, waits for them, and re-layouts, shards(): lax.dynamic_update_slice(act_all, block[:, None], (0, other, 0, 0, 0, 0))  9.34 us
    ppermute x6, starting transfers between devices, reduce_data(): piece = lax.ppermute(piece.astype(jnp.bfloat16), 'dp', pairs)  8.93 us
  transfers between devices with their start and end apart: 21, of which 9 were waited for; matrix products, arithmetic and copies ran while one was open for 42% of the time, Pallas kernels for 6%

profile of v1, /device:TPU:0, one launch (start us, length us, event | category | flops | bytes accessed | tf_op | source)
XLA Modules:
  0.0 224.2 jit_solution(1485668624117730974)
XLA Ops:
  10.2 5.5 %collective-permute-start.8 = (bf16[1,2,16,24,384]{4,3,2,1,0:T(8,128)(2,1)}, bf16[1,2,16,24,384]{4,3,2,1,0:T(8,128)(2,1)S(1)}, u32[]{:S(2)}, u32[]{:S(2)}) collective-permute-start(bf16[1,2,16,24,384]{4,3,2,1,0:T(8,128)(2,1)} %get-tuple-element.27), channel_id=1, source_target_pairs={{0,8},{8,16},{16,24},{1,9},{9,17},{17,25},{2,10},{10,18},{18,26},{... | collective-permute-start | bytes 1769480 | tf_op jit(solution)/shard_map/ppermute | solution.py:21
  15.8 7.9 %collective-permute-done = bf16[1,2,16,24,384]{4,3,2,1,0:T(8,128)(2,1)S(1)} collective-permute-done((bf16[1,2,16,24,384]{4,3,2,1,0:T(8,128)(2,1)S(1)}, bf16[1,2,16,24,384]{4,3,2,1,0:T(8,128)(2,1)S(1)}, u32[]{:S(2)}, u32[]{:S(2)}) %collective-permute-start) | collective-permute-done | bytes 589856 | tf_op jit(solution)/shard_map/ppermute | solution.py:21
  23.7 3.0 %collective-permute-start.2 = (bf16[1,2,16,24,384]{4,3,2,1,0:T(8,128)(2,1)}, bf16[1,2,16,24,384]{4,3,2,1,0:T(8,128)(2,1)}, u32[]{:S(2)}, u32[]{:S(2)}) collective-permute-start(bf16[1,2,16,24,384]{4,3,2,1,0:T(8,128)(2,1)} %get-tuple-element.27), channel_id=1, source_target_pairs={{0,8},{8,0},{16,24},{24,16},{1,9},{9,1},{17,25},{25,17},{2,10},{10... | collective-permute-start | bytes 1769480 | tf_op jit(solution)/shard_map/ppermute | solution.py:166
  32.8 3.2 %collective-permute-start.5 = (bf16[1,2,16,24,96]{4,3,2,1,0:T(8,128)(2,1)}, bf16[1,2,16,24,96]{4,3,2,1,0:T(8,128)(2,1)S(1)}, u32[]{:S(2)}, u32[]{:S(2)}) collective-permute-start(bf16[1,2,16,24,96]{4,3,2,1,0:T(8,128)(2,1)} %get-tuple-element.58), channel_id=1, source_target_pairs={{0,8},{8,0},{16,24},{24,16},{1,9},{9,1},{17,25},{25,17},{2,10},{10... | collective-permute-start | bytes 442376 | tf_op jit(solution)/shard_map/ppermute | solution.py:162
  41.2 18.7 %fusion.23 = f32[2,16,8,4,384]{4,2,3,1,0:T(8,128)S(1)} fusion(bf16[3,3,3,384,384]{4,3,2,1,0:T(8,128)(2,1)} %bitcast.154, bf16[4,16,1,7,2,384]{5,3,4,1,0,2:T(8,128)(2,1)S(1)} %slice.90, bf16[4,16,1,8,4,384]{5,3,4,1,0,2:T(8,128)(2,1)S(1)} %copy.30, pred[8,4]{0,1:T(4,128)(4,1)S(1)} %copy-done.17), kind=kOutput, calls=%fused_computation.35 | convolution fusion | flops 7821459456 | bytes 11796512 | tf_op jit(solution)/shard_map/conv_general_dilated | solution.py:176
  64.5 13.1 %collective-permute-done.5 = bf16[1,2,16,24,96]{4,3,2,1,0:T(8,128)(2,1)S(1)} collective-permute-done((bf16[1,2,16,24,96]{4,3,2,1,0:T(8,128)(2,1)}, bf16[1,2,16,24,96]{4,3,2,1,0:T(8,128)(2,1)S(1)}, u32[]{:S(2)}, u32[]{:S(2)}) %collective-permute-start.5) | collective-permute-done | bytes 147488 | tf_op jit(solution)/shard_map/ppermute | solution.py:162
  78.5 5.3 %collective-permute-done.6 = bf16[1,2,16,24,96]{4,3,2,1,0:T(8,128)(2,1)S(1)} collective-permute-done((bf16[1,2,16,24,96]{4,3,2,1,0:T(8,128)(2,1)S(1)}, bf16[1,2,16,24,96]{4,3,2,1,0:T(8,128)(2,1)S(1)}, u32[]{:S(2)}, u32[]{:S(2)}) %collective-permute-start.6) | collective-permute-done | bytes 147488 | tf_op jit(solution)/shard_map/ppermute | solution.py:162
  86.1 4.3 %collective-permute-done.7 = bf16[1,2,16,24,96]{4,3,2,1,0:T(8,128)(2,1)S(1)} collective-permute-done((bf16[1,2,16,24,96]{4,3,2,1,0:T(8,128)(2,1)S(1)}, bf16[1,2,16,24,96]{4,3,2,1,0:T(8,128)(2,1)S(1)}, u32[]{:S(2)}, u32[]{:S(2)}) %collective-permute-start.7) | collective-permute-done | bytes 147488 | tf_op jit(solution)/shard_map/ppermute | solution.py:162
  90.3 3.8 %collective-permute-start.9 = (bf16[1,2,16,24,384]{4,3,2,1,0:T(8,128)(2,1)}, bf16[1,2,16,24,384]{4,3,2,1,0:T(8,128)(2,1)}, u32[]{:S(2)}, u32[]{:S(2)}) collective-permute-start(bf16[1,2,16,24,384]{4,3,2,1,0:T(8,128)(2,1)} %fusion.45), channel_id=1, source_target_pairs={{0,8},{8,16},{16,24},{1,9},{9,17},{17,25},{2,10},{10,18},{18,26},{... | collective-permute-start | bytes 1769480 | tf_op jit(solution)/shard_map/ppermute | solution.py:21
  99.0 3.5 %copy.22 = bf16[1,4,2,16,24,384]{5,3,4,2,1,0:T(8,128)(2,1)} copy(bf16[1,4,2,16,24,384]{5,4,3,2,1,0:T(8,128)(2,1)} %bitcast_dynamic-update-slice_fusion) | data formatting | bytes 4718592 | tf_op jit(solution)/shard_map/dynamic_update_slice | solution.py:167
  104.5 4.3 %copy.28.left_ref = bf16[384,3072]{1,0:T(8,128)(2,1)} copy(bf16[384,3072]{0,1:T(8,128)(2,1)} %bitcast.10) | data formatting | bytes 4718592 | tf_op jit(solution)/shard_map/reshape | solution.py:83
  108.8 2.7 %convolution_bitcast_fusion.1 = f32[1152,384]{0,1:T(8,128)S(1)} fusion(bf16[1,2,16,24,384]{4,3,2,1,0:T(8,128)(2,1)} %fusion.45, bf16[1,2,16,24,384]{4,3,2,1,0:T(8,128)(2,1)} %collective-permute-done.9, bf16[1,4,16,24,384]{4,3,2,1,0:T(8,128)(2,1)} %param.11), kind=kOutput, calls=%fused_computation.6 | convolution fusion | flops 686555136 | bytes 3538944 | tf_op jit(solution)/shard_map/dot_general | solution.py:190
  111.5 2.4 %convolution_bitcast_fusion.2 = f32[1152,384]{0,1:T(8,128)S(1)} fusion(bf16[1,2,16,24,384]{4,3,2,1,0:T(8,128)(2,1)} %fusion.45, bf16[1,2,16,24,384]{4,3,2,1,0:T(8,128)(2,1)} %collective-permute-done.9, bf16[1,4,16,24,384]{4,3,2,1,0:T(8,128)(2,1)S(1)} %copy-done.15), kind=kOutput, calls=%fused_computation.7 | convolution fusion | flops 686555136 | bytes 3538944 | tf_op jit(solution)/shard_map/dot_general | solution.py:190
  116.7 13.6 %shard_map.72 = f32[3,9,384,96]{3,2,1,0:T(8,128)} custom-call(bf16[384,3072]{1,0:T(8,128)(2,1)S(1)} %copy-done.2, bf16[3,10,26,16,128]{4,3,2,1,0:T(8,128)(2,1)S(1)} %pad_maximum_fusion.1.right_ref), custom_call_target="tpu_custom_call" | custom-call | flops 8153726976 | bytes 9535488 | tf_op jit(solution)/shard_map/pallas_call | solution.py:89
  134.4 4.5 %constant_dynamic-slice_fusion.5 = (f32[4,1,1296,96]{3,2,1,0:T(8,128)}, f32[4,1,1296,96]{3,2,1,0:T(8,128)S(1)}) fusion(f32[4,2,1296,96]{3,2,1,0:T(8,128)} %bitcast.144, s32[]{:T(128)S(6)} %select_n.84, s32[]{:T(128)S(6)} %select_n.85), kind=kLoop, calls=%fused_computation.118 | loop fusion | bytes 7962632 | tf_op jit(solution)/shard_map/jit(dynamic_index_in_dim)/dynamic_slice | solution.py:41
  140.9 3.3 %copy.37 = f32[1152,768]{1,0:T(8,128)S(1)} copy(f32[1152,768]{0,1:T(8,128)} %pad_maximum_fusion) | data formatting | bytes 7077888 | tf_op jit(solution)/shard_map/optimization_barrier | solution.py:199
  147.6 13.6 %fusion.20 = f32[2,16,8,4,384]{4,2,3,1,0:T(8,128)S(1)} fusion(bf16[3,3,3,384,384]{4,3,2,1,0:T(8,128)(2,1)} %bitcast.155, bf16[4,16,1,7,2,384]{5,3,4,1,0,2:T(8,128)(2,1)S(1)} %copy-done.16, bf16[4,16,1,8,4,384]{5,3,4,1,0,2:T(8,128)(2,1)S(1)} %copy-done.12, pred[8,4]{0,1:T(4,128)(4,1)S(1)} %copy-done.17), kind=kOutput, calls=%fused_computation.34 | convolution fusion | flops 7821459456 | bytes 11796512 | tf_op jit(solution)/shard_map/conv_general_dilated | solution.py:208
  166.1 3.2 %copy.45 = f32[4,1,1296,96]{2,3,0,1:T(8,128)} copy(f32[4,1,1296,96]{3,2,1,0:T(8,128)} %get-tuple-element.36) | data formatting | bytes 3981312
  171.8 3.7 %collective-permute-start.17 = (bf16[144,768]{1,0:T(8,128)(2,1)S(1)}, bf16[144,768]{1,0:T(8,128)(2,1)S(1)}, u32[]{:S(2)}, u32[]{:S(2)}) collective-permute-start(bf16[144,768]{1,0:T(8,128)(2,1)S(1)} %get-tuple-element.45), channel_id=1, source_target_pairs={{0,6},{1,7},{2,4},{3,5},{4,2},{5,3},{6,0},{7,1},{8,14},{9,15},{10,... | collective-permute-start | bytes 663560 | tf_op jit(solution)/shard_map/ppermute | solution.py:49
  176.3 3.3 %bitcast_add_fusion = f32[4,1296,96]{1,2,0:T(8,128)} fusion(f32[4,1296,96]{1,2,0:T(8,128)} %collective-permute-done.10, f32[4,1,1296,96]{2,3,0,1:T(8,128)S(1)} %copy-done.6), kind=kLoop, calls=%fused_computation.20 | loop fusion | flops 497664 | bytes 5971968 | tf_op jit(solution)/shard_map/add | solution.py:43
  179.5 2.5 %collective-permute-done.17 = bf16[144,768]{1,0:T(8,128)(2,1)S(1)} collective-permute-done((bf16[144,768]{1,0:T(8,128)(2,1)S(1)}, bf16[144,768]{1,0:T(8,128)(2,1)S(1)}, u32[]{:S(2)}, u32[]{:S(2)}) %collective-permute-start.17) | collective-permute-done | bytes 221216 | tf_op jit(solution)/shard_map/ppermute | solution.py:49
  182.0 12.9 %collective-permute-done.16 = bf16[144,768]{1,0:T(8,128)(2,1)S(1)} collective-permute-done((bf16[144,768]{1,0:T(8,128)(2,1)S(1)}, bf16[144,768]{1,0:T(8,128)(2,1)S(1)}, u32[]{:S(2)}, u32[]{:S(2)}) %collective-permute-start.16) | collective-permute-done | bytes 221216 | tf_op jit(solution)/shard_map/ppermute | solution.py:49
  197.6 2.5 %collective-permute-start.13 = (bf16[1296,96]{0,1:T(8,128)(2,1)S(1)}, bf16[1296,96]{0,1:T(8,128)(2,1)S(1)}, u32[]{:S(2)}, u32[]{:S(2)}) collective-permute-start(bf16[1296,96]{0,1:T(8,128)(2,1)S(1)} %get-tuple-element.42), channel_id=1, source_target_pairs={{0,6},{1,7},{2,4},{3,5},{4,2},{5,3},{6,0},{7,1},{8,14},{9,15},{10,... | collective-permute-start | bytes 746504 | tf_op jit(solution)/shard_map/ppermute | solution.py:49
  209.6 12.6 %collective-permute-done.12 = bf16[1296,96]{0,1:T(8,128)(2,1)S(1)} collective-permute-done((bf16[1296,96]{0,1:T(8,128)(2,1)S(1)}, bf16[1296,96]{0,1:T(8,128)(2,1)S(1)}, u32[]{:S(2)}, u32[]{:S(2)}) %collective-permute-start.12) | collective-permute-done | bytes 248864 | tf_op jit(solution)/shard_map/ppermute | solution.py:49
  (137 shorter events, 69.9 us)
Async XLA Ops:
  4.4 23.7 %copy-start.7 = (f32[1,1,16,24,384]{4,3,2,1,0:T(8,128)}, f32[1,1,16,24,384]{4,3,2,1,0:T(8,128)S(1)}, u32[]{:S(2)}) copy-start(f32[1,1,16,24,384]{4,3,2,1,0:T(8,128)S(1)} %get-tuple-element.38) | copy-start | bytes 1769476
  4.4 23.7 %copy-start.9 = (f32[1,1,16,24,384]{4,3,2,1,0:T(8,128)}, f32[1,1,16,24,384]{4,3,2,1,0:T(8,128)S(1)}, u32[]{:S(2)}) copy-start(f32[1,1,16,24,384]{4,3,2,1,0:T(8,128)S(1)} %get-tuple-element.39) | copy-start | bytes 1769476
  4.5 19.1 %collective-permute-start = (bf16[1,2,16,24,384]{4,3,2,1,0:T(8,128)(2,1)S(1)}, bf16[1,2,16,24,384]{4,3,2,1,0:T(8,128)(2,1)S(1)}, u32[]{:S(2)}, u32[]{:S(2)}) collective-permute-start(bf16[1,2,16,24,384]{4,3,2,1,0:T(8,128)(2,1)S(1)} %pad_maximum_fusion.4), channel_id=1, source_target_pairs={{8,0},{16,8},{24,16},{9,1},{17,9},{25,17},{10,2},{18,10},{26,18},{... | collective-permute-start | bytes 1769480 | tf_op jit(solution)/shard_map/ppermute | solution.py:21
  10.2 22.6 %collective-permute-start.8 = (bf16[1,2,16,24,384]{4,3,2,1,0:T(8,128)(2,1)}, bf16[1,2,16,24,384]{4,3,2,1,0:T(8,128)(2,1)S(1)}, u32[]{:S(2)}, u32[]{:S(2)}) collective-permute-start(bf16[1,2,16,24,384]{4,3,2,1,0:T(8,128)(2,1)} %get-tuple-element.27), channel_id=1, source_target_pairs={{0,8},{8,16},{16,24},{1,9},{9,17},{17,25},{2,10},{10,18},{18,26},{... | collective-permute-start | bytes 1769480 | tf_op jit(solution)/shard_map/ppermute | solution.py:21
  23.7 71.5 %collective-permute-start.2 = (bf16[1,2,16,24,384]{4,3,2,1,0:T(8,128)(2,1)}, bf16[1,2,16,24,384]{4,3,2,1,0:T(8,128)(2,1)}, u32[]{:S(2)}, u32[]{:S(2)}) collective-permute-start(bf16[1,2,16,24,384]{4,3,2,1,0:T(8,128)(2,1)} %get-tuple-element.27), channel_id=1, source_target_pairs={{0,8},{8,0},{16,24},{24,16},{1,9},{9,1},{17,25},{25,17},{2,10},{10... | collective-permute-start | bytes 1769480 | tf_op jit(solution)/shard_map/ppermute | solution.py:166
  26.6 70.5 %collective-permute-start.3 = (bf16[1,2,16,24,384]{4,3,2,1,0:T(8,128)(2,1)}, bf16[1,2,16,24,384]{4,3,2,1,0:T(8,128)(2,1)}, u32[]{:S(2)}, u32[]{:S(2)}) collective-permute-start(bf16[1,2,16,24,384]{4,3,2,1,0:T(8,128)(2,1)} %get-tuple-element.27), channel_id=1, source_target_pairs={{0,16},{8,24},{16,0},{24,8},{1,17},{9,25},{17,1},{25,9},{2,18},{10... | collective-permute-start | bytes 1769480 | tf_op jit(solution)/shard_map/ppermute | solution.py:166
  26.6 75.9 %collective-permute-start.4 = (bf16[1,2,16,24,384]{4,3,2,1,0:T(8,128)(2,1)}, bf16[1,2,16,24,384]{4,3,2,1,0:T(8,128)(2,1)}, u32[]{:S(2)}, u32[]{:S(2)}) collective-permute-start(bf16[1,2,16,24,384]{4,3,2,1,0:T(8,128)(2,1)} %get-tuple-element.27), channel_id=1, source_target_pairs={{0,24},{8,16},{16,8},{24,0},{1,25},{9,17},{17,9},{25,1},{2,26},{10... | collective-permute-start | bytes 1769480 | tf_op jit(solution)/shard_map/ppermute | solution.py:166
  29.0 101.2 %collective-permute-start.1 = (bf16[1,2,16,24,384]{4,3,2,1,0:T(8,128)(2,1)}, bf16[1,2,16,24,384]{4,3,2,1,0:T(8,128)(2,1)}, u32[]{:S(2)}, u32[]{:S(2)}) collective-permute-start(bf16[1,2,16,24,384]{4,3,2,1,0:T(8,128)(2,1)} %fusion.54), channel_id=1, source_target_pairs={{8,0},{16,8},{24,16},{9,1},{17,9},{25,17},{10,2},{18,10},{26,18},{... | collective-permute-start | bytes 1769480 | tf_op jit(solution)/shard_map/ppermute | solution.py:21
  32.8 44.8 %collective-permute-start.5 = (bf16[1,2,16,24,96]{4,3,2,1,0:T(8,128)(2,1)}, bf16[1,2,16,24,96]{4,3,2,1,0:T(8,128)(2,1)S(1)}, u32[]{:S(2)}, u32[]{:S(2)}) collective-permute-start(bf16[1,2,16,24,96]{4,3,2,1,0:T(8,128)(2,1)} %get-tuple-element.58), channel_id=1, source_target_pairs={{0,8},{8,0},{16,24},{24,16},{1,9},{9,1},{17,25},{25,17},{2,10},{10... | collective-permute-start | bytes 442376 | tf_op jit(solution)/shard_map/ppermute | solution.py:162
  77.6 6.1 %collective-permute-start.6 = (bf16[1,2,16,24,96]{4,3,2,1,0:T(8,128)(2,1)S(1)}, bf16[1,2,16,24,96]{4,3,2,1,0:T(8,128)(2,1)S(1)}, u32[]{:S(2)}, u32[]{:S(2)}) collective-permute-start(bf16[1,2,16,24,96]{4,3,2,1,0:T(8,128)(2,1)S(1)} %get-tuple-element.57), channel_id=1, source_target_pairs={{0,16},{8,24},{16,0},{24,8},{1,17},{9,25},{17,1},{25,9},{2,18},{10... | collective-permute-start | bytes 442376 | tf_op jit(solution)/shard_map/ppermute | solution.py:162
  83.7 6.6 %collective-permute-start.7 = (bf16[1,2,16,24,96]{4,3,2,1,0:T(8,128)(2,1)S(1)}, bf16[1,2,16,24,96]{4,3,2,1,0:T(8,128)(2,1)S(1)}, u32[]{:S(2)}, u32[]{:S(2)}) collective-permute-start(bf16[1,2,16,24,96]{4,3,2,1,0:T(8,128)(2,1)S(1)} %get-tuple-element.56), channel_id=1, source_target_pairs={{0,24},{8,16},{16,8},{24,0},{1,25},{9,17},{17,9},{25,1},{2,26},{10... | collective-permute-start | bytes 442376 | tf_op jit(solution)/shard_map/ppermute | solution.py:162
  90.3 18.5 %collective-permute-start.9 = (bf16[1,2,16,24,384]{4,3,2,1,0:T(8,128)(2,1)}, bf16[1,2,16,24,384]{4,3,2,1,0:T(8,128)(2,1)}, u32[]{:S(2)}, u32[]{:S(2)}) collective-permute-start(bf16[1,2,16,24,384]{4,3,2,1,0:T(8,128)(2,1)} %fusion.45), channel_id=1, source_target_pairs={{0,8},{8,16},{16,24},{1,9},{9,17},{17,25},{2,10},{10,18},{18,26},{... | collective-permute-start | bytes 1769480 | tf_op jit(solution)/shard_map/ppermute | solution.py:21
  140.9 35.3 %collective-permute-start.10 = (f32[4,1296,96]{1,2,0:T(8,128)}, f32[4,1296,96]{1,2,0:T(8,128)}, u32[]{:S(2)}, u32[]{:S(2)}) collective-permute-start(f32[4,1296,96]{1,2,0:T(8,128)} %bitcast.147), channel_id=1, source_target_pairs={{0,1},{1,0},{2,3},{3,2},{4,5},{5,4},{6,7},{7,6},{8,9},{9,8},{10,11... | collective-permute-start | bytes 5971976 | tf_op jit(solution)/shard_map/ppermute | solution.py:43
  145.7 23.6 %collective-permute-start.14 = (f32[4,144,768]{2,1,0:T(8,128)}, f32[4,144,768]{2,1,0:T(8,128)}, u32[]{:S(2)}, u32[]{:S(2)}) collective-permute-start(f32[4,144,768]{2,1,0:T(8,128)} %dynamic-slice_bitcast_fusion), channel_id=1, source_target_pairs={{0,1},{1,0},{2,3},{3,2},{4,5},{5,4},{6,7},{7,6},{8,9},{9,8},{10,11... | collective-permute-start | bytes 5308424 | tf_op jit(solution)/shard_map/ppermute | solution.py:43
  171.8 10.2 %collective-permute-start.17 = (bf16[144,768]{1,0:T(8,128)(2,1)S(1)}, bf16[144,768]{1,0:T(8,128)(2,1)S(1)}, u32[]{:S(2)}, u32[]{:S(2)}) collective-permute-start(bf16[144,768]{1,0:T(8,128)(2,1)S(1)} %get-tuple-element.45), channel_id=1, source_target_pairs={{0,6},{1,7},{2,4},{3,5},{4,2},{5,3},{6,0},{7,1},{8,14},{9,15},{10,... | collective-permute-start | bytes 663560 | tf_op jit(solution)/shard_map/ppermute | solution.py:49
  175.5 19.5 %collective-permute-start.16 = (bf16[144,768]{1,0:T(8,128)(2,1)S(1)}, bf16[144,768]{1,0:T(8,128)(2,1)S(1)}, u32[]{:S(2)}, u32[]{:S(2)}) collective-permute-start(bf16[144,768]{1,0:T(8,128)(2,1)S(1)} %get-tuple-element.46), channel_id=1, source_target_pairs={{0,4},{1,5},{2,6},{3,7},{4,0},{5,1},{6,2},{7,3},{8,12},{9,13},{10,... | collective-permute-start | bytes 663560 | tf_op jit(solution)/shard_map/ppermute | solution.py:49
  175.5 19.5 %collective-permute-start.15 = (bf16[144,768]{1,0:T(8,128)(2,1)S(1)}, bf16[144,768]{1,0:T(8,128)(2,1)S(1)}, u32[]{:S(2)}, u32[]{:S(2)}) collective-permute-start(bf16[144,768]{1,0:T(8,128)(2,1)S(1)} %get-tuple-element.44), channel_id=1, source_target_pairs={{0,2},{1,3},{2,0},{3,1},{4,6},{5,7},{6,4},{7,5},{8,10},{9,11},{10,... | collective-permute-start | bytes 663560 | tf_op jit(solution)/shard_map/ppermute | solution.py:49
  196.0 7.6 %collective-permute-start.20 = (f32[144,192]{1,0:T(8,128)S(1)}, f32[144,192]{1,0:T(8,128)S(1)}, u32[]{:S(2)}, u32[]{:S(2)}) collective-permute-start(f32[144,192]{1,0:T(8,128)S(1)} %bitcast.151), channel_id=1, source_target_pairs={{0,24},{8,16},{16,8},{24,0},{1,25},{9,17},{17,9},{25,1},{2,26},{10... | collective-permute-start | bytes 331784 | tf_op jit(solution)/shard_map/ppermute | solution.py:31
  197.6 12.0 %collective-permute-start.13 = (bf16[1296,96]{0,1:T(8,128)(2,1)S(1)}, bf16[1296,96]{0,1:T(8,128)(2,1)S(1)}, u32[]{:S(2)}, u32[]{:S(2)}) collective-permute-start(bf16[1296,96]{0,1:T(8,128)(2,1)S(1)} %get-tuple-element.42), channel_id=1, source_target_pairs={{0,6},{1,7},{2,4},{3,5},{4,2},{5,3},{6,0},{7,1},{8,14},{9,15},{10,... | collective-permute-start | bytes 746504 | tf_op jit(solution)/shard_map/ppermute | solution.py:49
  200.1 22.1 %collective-permute-start.12 = (bf16[1296,96]{0,1:T(8,128)(2,1)S(1)}, bf16[1296,96]{0,1:T(8,128)(2,1)S(1)}, u32[]{:S(2)}, u32[]{:S(2)}) collective-permute-start(bf16[1296,96]{0,1:T(8,128)(2,1)S(1)} %get-tuple-element.43), channel_id=1, source_target_pairs={{0,4},{1,5},{2,6},{3,7},{4,0},{5,1},{6,2},{7,3},{8,12},{9,13},{10,... | collective-permute-start | bytes 746504 | tf_op jit(solution)/shard_map/ppermute | solution.py:49
  200.1 22.1 %collective-permute-start.11 = (bf16[1296,96]{0,1:T(8,128)(2,1)S(1)}, bf16[1296,96]{0,1:T(8,128)(2,1)S(1)}, u32[]{:S(2)}, u32[]{:S(2)}) collective-permute-start(bf16[1296,96]{0,1:T(8,128)(2,1)S(1)} %get-tuple-element.41), channel_id=1, source_target_pairs={{0,2},{1,3},{2,0},{3,1},{4,6},{5,7},{6,4},{7,5},{8,10},{9,11},{10,... | collective-permute-start | bytes 746504 | tf_op jit(solution)/shard_map/ppermute | solution.py:49
  202.0 5.2 %collective-permute-start.19 = (f32[144,192]{1,0:T(8,128)S(1)}, f32[144,192]{1,0:T(8,128)S(1)}, u32[]{:S(2)}, u32[]{:S(2)}) collective-permute-start(f32[144,192]{1,0:T(8,128)S(1)} %bitcast.152), channel_id=1, source_target_pairs={{0,16},{8,24},{16,0},{24,8},{1,17},{9,25},{17,1},{25,9},{2,18},{10... | collective-permute-start | bytes 331784 | tf_op jit(solution)/shard_map/ppermute | solution.py:31
  203.7 5.2 %collective-permute-start.18 = (f32[144,192]{1,0:T(8,128)S(1)}, f32[144,192]{1,0:T(8,128)S(1)}, u32[]{:S(2)}, u32[]{:S(2)}) collective-permute-start(f32[144,192]{1,0:T(8,128)S(1)} %bitcast.153), channel_id=1, source_target_pairs={{0,8},{8,0},{16,24},{24,16},{1,9},{9,1},{17,25},{25,17},{2,10},{10... | collective-permute-start | bytes 331784 | tf_op jit(solution)/shard_map/ppermute | solution.py:31
  205.7 18.5 %copy-start.1 = (bf16[1152,768]{1,0:T(8,128)(2,1)S(1)}, bf16[1152,768]{1,0:T(8,128)(2,1)}, u32[]{:S(2)}) copy-start(bf16[1152,768]{1,0:T(8,128)(2,1)} %param.10) | copy-start | bytes 5308420
  (15 other events, 83.7 us)

commit v2 on v1

--- a/solution.py
+++ b/solution.py
@@ -32,7 +32,7 @@
     return total
 
 
-def reduce_data(part):
+def pair_sum(part):
     count = lax.axis_size("dp")
     me = lax.axis_index("dp")
     rows = part.shape[0] // count
@@ -40,7 +40,12 @@
     core = me % 2
     kept = lax.dynamic_index_in_dim(blocks, core, 1, keepdims=False)
     sent = lax.dynamic_index_in_dim(blocks, 1 - core, 1, keepdims=False)
-    pair = kept + lax.ppermute(sent, "dp", [(place, place ^ 1) for place in range(count)])
+    return kept + lax.ppermute(sent, "dp", [(place, place ^ 1) for place in range(count)])
+
+
+def reduce_pairs(pair):
+    count = lax.axis_size("dp")
+    me = lax.axis_index("dp")
     home = me // 2
     total = lax.dynamic_index_in_dim(pair, home, 0, keepdims=False)
     for step in range(1, count // 2):
@@ -197,10 +202,10 @@
     ]
     conv_ext = jnp.concatenate([conv_grad, conv_next], axis=1)
     conv_ext, conv_part, up_part = lax.optimization_barrier(
-        (conv_ext, conv_part, jnp.concatenate(halves, axis=1))
-    )
-    grad_conv = reduce_data(conv_part) * scale
-    up_part = reduce_data(up_part)
+        (conv_ext, pair_sum(conv_part), pair_sum(jnp.concatenate(halves, axis=1)))
+    )
+    grad_conv = reduce_pairs(conv_part) * scale
+    up_part = reduce_pairs(up_part)
     up_width = 2 * channels // time_count
     up_part = up_part.reshape(-1, time_count, up_width).transpose(1, 0, 2)
     grad_up = exchange(up_part, "tm", jnp.float32) * scale

time: 225 us -> 237 us (1.053)
  starting transfers between devices: 35.9 us -> 57.2 us
  waiting for transfers between devices: 60.5 us -> 40.8 us
  local copies, waits for them, and re-layouts: 53.3 us -> 58.8 us
  other arithmetic: 20.6 us -> 25.3 us
    ppermute x3, waiting for transfers between devices: 22.7 us -> 0.78 us  [shards(): piece = lax.ppermute(piece, 'tm', pairs)]
    ppermute x8, starting transfers between devices: 9.44 us -> 28.9 us  [the longest x6 28.4 us: reduce_pairs(): piece = lax.ppermute(piece.astype(jnp.bfloat16), 'dp', pairs)]
    ppermute x4, waiting for transfers between devices: 7.88 us -> 22.5 us  [from_behind(): lax.ppermute(value, axis, [(source, source + steps) for source in range(f...]
    ppermute x8, waiting for transfers between devices: 28 us -> 14.6 us  [the longest x6 14.6 us: reduce_pairs(): piece = lax.ppermute(piece.astype(jnp.bfloat16), 'dp', pairs)]
    unnamed x41 -> x33, local copies, waits for them, and re-layouts: 7.99 us -> 0.43 us
    dynamic_slice x1 -> x3, local copies, waits for them, and re-layouts: 4.46 us -> 9.8 us  [the longest x2 7.77 us: pair_sum(): kept = lax.dynamic_index_in_dim(blocks, core, 1, keepdims=False)]
    concatenate x0 -> x1, local copies, waits for them, and re-layouts: none -> 5.24 us  [shards(): jnp.concatenate(halves, axis=1)]
    optimization_barrier x2 -> x1, local copies, waits for them, and re-layouts: 3.98 us -> 0.68 us  [shards(): lax.optimization_barrier((conv_ext, pair_sum(conv_part), pair_sum(jnp.con...]
  transfers between devices with their start and end apart: 21 -> 21, of which waited for: 9 -> 8; matrix products, arithmetic and copies ran while one was open for 42% -> 31% of each run, Pallas kernels for 6% -> 6%
where the time goes in v2:
time: 237 us; the launch traced here: 236 us
  local copies, waits for them, and re-layouts  58.8 us (25%)
  starting transfers between devices  57.2 us (24%)
  waiting for transfers between devices  40.8 us (17%)
  matrix products  39.2 us (17%)
  other arithmetic  25.3 us (11%)
  Pallas kernels  13.5 us (6%)
    ppermute x6, starting transfers between devices, reduce_pairs(): piece = lax.ppermute(piece.astype(jnp.bfloat16), 'dp', pairs)  28.4 us
    ppermute x4, waiting for transfers between devices, from_behind(): lax.ppermute(value, axis, [(source, source + steps) for source in range(f...  22.5 us
    conv_general_dilated x1, matrix products, shards(): lax.conv_general_dilated(jnp.concatenate([act_prior, act], axis=1), kerne...  18.7 us
    ppermute x6, waiting for transfers between devices, reduce_pairs(): piece = lax.ppermute(piece.astype(jnp.bfloat16), 'dp', pairs)  14.6 us
    conv_general_dilated x1, matrix products, shards(): lax.conv_general_dilated(conv_ext, lax.rev(kernel, (0, 1, 2)), (1, 1, 1),...  13.6 us
    pallas_call x1, Pallas kernels, weight_gradient(): pl.pallas_call(functools.partial(weight_body, frames, breadth), grid=(9,)...  13.5 us
    ppermute x4, starting transfers between devices, from_behind(): lax.ppermute(value, axis, [(source, source + steps) for source in range(f...  12 us
    dynamic_update_slice x4, local copies, waits for them, and re-layouts, shards(): lax.dynamic_update_slice(act_all, block[:, None], (0, other, 0, 0, 0, 0))  9.3 us
  transfers between devices with their start and end apart: 21, of which 8 were waited for; matrix products, arithmetic and copies ran while one was open for 31% of the time, Pallas kernels for 6%

profile of v2, /device:TPU:0, one launch (start us, length us, event | category | flops | bytes accessed | tf_op | source)
XLA Modules:
  0.0 236.1 jit_solution(2127536042234472939)
XLA Ops:
  10.2 5.7 %collective-permute-start.9 = (bf16[1,2,16,24,384]{4,3,2,1,0:T(8,128)(2,1)}, bf16[1,2,16,24,384]{4,3,2,1,0:T(8,128)(2,1)S(1)}, u32[]{:S(2)}, u32[]{:S(2)}) collective-permute-start(bf16[1,2,16,24,384]{4,3,2,1,0:T(8,128)(2,1)} %get-tuple-element.27), channel_id=1, source_target_pairs={{0,8},{8,16},{16,24},{1,9},{9,17},{17,25},{2,10},{10,18},{18,26},{... | collective-permute-start | bytes 1769480 | tf_op jit(solution)/shard_map/ppermute | solution.py:21
  16.0 7.7 %collective-permute-done = bf16[1,2,16,24,384]{4,3,2,1,0:T(8,128)(2,1)S(1)} collective-permute-done((bf16[1,2,16,24,384]{4,3,2,1,0:T(8,128)(2,1)S(1)}, bf16[1,2,16,24,384]{4,3,2,1,0:T(8,128)(2,1)S(1)}, u32[]{:S(2)}, u32[]{:S(2)}) %collective-permute-start) | collective-permute-done | bytes 589856 | tf_op jit(solution)/shard_map/ppermute | solution.py:21
  23.7 3.0 %collective-permute-start.2 = (bf16[1,2,16,24,384]{4,3,2,1,0:T(8,128)(2,1)}, bf16[1,2,16,24,384]{4,3,2,1,0:T(8,128)(2,1)}, u32[]{:S(2)}, u32[]{:S(2)}) collective-permute-start(bf16[1,2,16,24,384]{4,3,2,1,0:T(8,128)(2,1)} %get-tuple-element.27), channel_id=1, source_target_pairs={{0,8},{8,0},{16,24},{24,16},{1,9},{9,1},{17,25},{25,17},{2,10},{10... | collective-permute-start | bytes 1769480 | tf_op jit(solution)/shard_map/ppermute | solution.py:171
  33.3 4.5 %collective-permute-start.6 = (bf16[1,2,16,24,96]{4,3,2,1,0:T(8,128)(2,1)S(1)}, bf16[1,2,16,24,96]{4,3,2,1,0:T(8,128)(2,1)S(1)}, u32[]{:S(2)}, u32[]{:S(2)}) collective-permute-start(bf16[1,2,16,24,96]{4,3,2,1,0:T(8,128)(2,1)S(1)} %get-tuple-element.57), channel_id=1, source_target_pairs={{0,16},{8,24},{16,0},{24,8},{1,17},{9,25},{17,1},{25,9},{2,18},{10... | collective-permute-start | bytes 442376 | tf_op jit(solution)/shard_map/ppermute | solution.py:167
  43.0 18.7 %fusion.23 = f32[2,16,8,4,384]{4,2,3,1,0:T(8,128)S(1)} fusion(bf16[3,3,3,384,384]{4,3,2,1,0:T(8,128)(2,1)} %bitcast.152, bf16[4,16,1,7,2,384]{5,3,4,1,0,2:T(8,128)(2,1)S(1)} %slice.90, bf16[4,16,1,8,4,384]{5,3,4,1,0,2:T(8,128)(2,1)S(1)} %copy.32, pred[8,4]{0,1:T(4,128)(4,1)S(1)} %copy-done.14), kind=kOutput, calls=%fused_computation.35 | convolution fusion | flops 7821459456 | bytes 11796512 | tf_op jit(solution)/shard_map/conv_general_dilated | solution.py:181
  68.7 3.3 %collective-permute-start.10 = (bf16[1,2,16,24,384]{4,3,2,1,0:T(8,128)(2,1)}, bf16[1,2,16,24,384]{4,3,2,1,0:T(8,128)(2,1)}, u32[]{:S(2)}, u32[]{:S(2)}) collective-permute-start(bf16[1,2,16,24,384]{4,3,2,1,0:T(8,128)(2,1)} %fusion.45), channel_id=1, source_target_pairs={{0,8},{8,16},{16,24},{1,9},{9,17},{17,25},{2,10},{10,18},{18,26},{... | collective-permute-start | bytes 1769480 | tf_op jit(solution)/shard_map/ppermute | solution.py:21
  77.8 3.4 %copy.22 = bf16[1,4,2,16,24,384]{5,3,4,2,1,0:T(8,128)(2,1)} copy(bf16[1,4,2,16,24,384]{5,4,3,2,1,0:T(8,128)(2,1)} %bitcast_dynamic-update-slice_fusion) | data formatting | bytes 4718592 | tf_op jit(solution)/shard_map/dynamic_update_slice | solution.py:172
  83.2 4.3 %copy.28.left_ref = bf16[384,3072]{1,0:T(8,128)(2,1)} copy(bf16[384,3072]{0,1:T(8,128)(2,1)} %bitcast.10) | data formatting | bytes 4718592 | tf_op jit(solution)/shard_map/reshape | solution.py:88
  87.5 2.7 %convolution_bitcast_fusion.1 = f32[1152,384]{0,1:T(8,128)S(1)} fusion(bf16[1,2,16,24,384]{4,3,2,1,0:T(8,128)(2,1)} %fusion.45, bf16[1,2,16,24,384]{4,3,2,1,0:T(8,128)(2,1)} %collective-permute-done.10, bf16[1,4,16,24,384]{4,3,2,1,0:T(8,128)(2,1)} %param.11), kind=kOutput, calls=%fused_computation.6 | convolution fusion | flops 686555136 | bytes 3538944 | tf_op jit(solution)/shard_map/dot_general | solution.py:195
  90.2 2.4 %convolution_bitcast_fusion.2 = f32[1152,384]{0,1:T(8,128)S(1)} fusion(bf16[1,2,16,24,384]{4,3,2,1,0:T(8,128)(2,1)} %fusion.45, bf16[1,2,16,24,384]{4,3,2,1,0:T(8,128)(2,1)} %collective-permute-done.10, bf16[1,4,16,24,384]{4,3,2,1,0:T(8,128)(2,1)S(1)} %copy-done.13), kind=kOutput, calls=%fused_computation.7 | convolution fusion | flops 686555136 | bytes 3538944 | tf_op jit(solution)/shard_map/dot_general | solution.py:195
  94.6 5.2 %copy.34 = f32[1152,768]{1,0:T(8,128)} copy(f32[1152,768]{0,1:T(8,128)} %pad_maximum_fusion) | data formatting | bytes 7077888 | tf_op jit(solution)/shard_map/concatenate | solution.py:205
  99.8 2.9 %dynamic-slice_bitcast_fusion = f32[4,144,768]{2,1,0:T(8,128)} fusion(f32[4,2,144,768]{3,2,1,0:T(8,128)} %bitcast.141, s32[]{:T(128)S(6)} %select_n.85), kind=kLoop, calls=%fused_computation.30 | loop fusion | bytes 3538948 | tf_op jit(solution)/shard_map/jit(dynamic_index_in_dim)/squeeze | solution.py:42
  102.8 13.5 %shard_map.72 = f32[3,9,384,96]{3,2,1,0:T(8,128)} custom-call(bf16[384,3072]{1,0:T(8,128)(2,1)S(1)} %copy-done.2, bf16[3,10,26,16,128]{4,3,2,1,0:T(8,128)(2,1)S(1)} %pad_maximum_fusion.1.right_ref), custom_call_target="tpu_custom_call" | custom-call | flops 8153726976 | bytes 9535488 | tf_op jit(solution)/shard_map/pallas_call | solution.py:94
  116.3 4.4 %constant_dynamic-slice_fusion.5 = (f32[4,1,1296,96]{3,2,1,0:T(8,128)}, f32[4,1,1296,96]{3,2,1,0:T(8,128)S(1)}) fusion(f32[4,2,1296,96]{3,2,1,0:T(8,128)} %bitcast.143, s32[]{:T(128)S(6)} %select_n.84, s32[]{:T(128)S(6)} %select_n.85), kind=kLoop, calls=%fused_computation.118 | loop fusion | bytes 7962632 | tf_op jit(solution)/shard_map/jit(dynamic_index_in_dim)/dynamic_slice | solution.py:41
  124.8 3.4 %copy.29 = f32[4,1,1296,96]{2,3,0,1:T(8,128)} copy(f32[4,1,1296,96]{3,2,1,0:T(8,128)} %get-tuple-element.36) | data formatting | bytes 3981312 | tf_op jit(solution)/shard_map/jit(dynamic_index_in_dim)/dynamic_slice | solution.py:41
  128.2 14.8 %collective-permute-done.1 = bf16[1,2,16,24,384]{4,3,2,1,0:T(8,128)(2,1)} collective-permute-done((bf16[1,2,16,24,384]{4,3,2,1,0:T(8,128)(2,1)}, bf16[1,2,16,24,384]{4,3,2,1,0:T(8,128)(2,1)}, u32[]{:S(2)}, u32[]{:S(2)}) %collective-permute-start.1) | collective-permute-done | bytes 589856 | tf_op jit(solution)/shard_map/ppermute | solution.py:21
  144.4 3.1 %bitcast_add_fusion.1 = f32[4,144,768]{2,1,0:T(8,128)} fusion(f32[4,144,768]{2,1,0:T(8,128)} %collective-permute-done.11, f32[4,2,144,768]{3,2,1,0:T(8,128)S(1)} %bitcast.142, s32[]{:T(128)S(6)} %select_n.84), kind=kLoop, calls=%fused_computation.29 | loop fusion | flops 442368 | bytes 5308420 | tf_op jit(solution)/shard_map/add | solution.py:43
  147.5 3.3 %bitcast_add_fusion = f32[4,1296,96]{1,2,0:T(8,128)} fusion(f32[4,1296,96]{1,2,0:T(8,128)} %collective-permute-done.8, f32[4,1,1296,96]{2,3,0,1:T(8,128)S(1)} %copy-done.6), kind=kLoop, calls=%fused_computation.20 | loop fusion | flops 497664 | bytes 5971968 | tf_op jit(solution)/shard_map/add | solution.py:43
  152.4 13.6 %fusion.20 = f32[2,16,8,4,384]{4,2,3,1,0:T(8,128)S(1)} fusion(bf16[3,3,3,384,384]{4,3,2,1,0:T(8,128)(2,1)} %bitcast.153, bf16[4,16,1,7,2,384]{5,3,4,1,0,2:T(8,128)(2,1)S(1)} %slice.92, bf16[4,16,1,8,4,384]{5,3,4,1,0,2:T(8,128)(2,1)S(1)} %copy.36, pred[8,4]{0,1:T(4,128)(4,1)S(1)} %copy-done.14), kind=kOutput, calls=%fused_computation.34 | convolution fusion | flops 7821459456 | bytes 11796512 | tf_op jit(solution)/shard_map/conv_general_dilated | solution.py:213
  178.5 3.6 %collective-permute-start.14 = (bf16[1296,96]{0,1:T(8,128)(2,1)}, bf16[1296,96]{0,1:T(8,128)(2,1)}, u32[]{:S(2)}, u32[]{:S(2)}) collective-permute-start(bf16[1296,96]{0,1:T(8,128)(2,1)} %get-tuple-element.42), channel_id=1, source_target_pairs={{0,6},{1,7},{2,4},{3,5},{4,2},{5,3},{6,0},{7,1},{8,14},{9,15},{10,... | collective-permute-start | bytes 746504 | tf_op jit(solution)/shard_map/ppermute | solution.py:54
  189.2 11.3 %collective-permute-done.17 = bf16[144,768]{1,0:T(8,128)(2,1)S(1)} collective-permute-done((bf16[144,768]{1,0:T(8,128)(2,1)S(1)}, bf16[144,768]{1,0:T(8,128)(2,1)S(1)}, u32[]{:S(2)}, u32[]{:S(2)}) %collective-permute-start.17) | collective-permute-done | bytes 221216 | tf_op jit(solution)/shard_map/ppermute | solution.py:54
  200.5 20.3 %collective-permute-start.12 = (bf16[1296,96]{0,1:T(8,128)(2,1)}, bf16[1296,96]{0,1:T(8,128)(2,1)S(1)}, u32[]{:S(2)}, u32[]{:S(2)}) collective-permute-start(bf16[1296,96]{0,1:T(8,128)(2,1)} %get-tuple-element.41), channel_id=1, source_target_pairs={{0,2},{1,3},{2,0},{3,1},{4,6},{5,7},{6,4},{7,5},{8,10},{9,11},{10,... | collective-permute-start | bytes 746504 | tf_op jit(solution)/shard_map/ppermute | solution.py:54
  220.8 3.3 %collective-permute-done.16 = bf16[144,768]{1,0:T(8,128)(2,1)S(1)} collective-permute-done((bf16[144,768]{1,0:T(8,128)(2,1)S(1)}, bf16[144,768]{1,0:T(8,128)(2,1)S(1)}, u32[]{:S(2)}, u32[]{:S(2)}) %collective-permute-start.16) | collective-permute-done | bytes 221216 | tf_op jit(solution)/shard_map/ppermute | solution.py:54
  226.3 3.8 %collective-permute-start.19 = (f32[144,192]{1,0:T(8,128)S(1)}, f32[144,192]{1,0:T(8,128)S(1)}, u32[]{:S(2)}, u32[]{:S(2)}) collective-permute-start(f32[144,192]{1,0:T(8,128)S(1)} %bitcast.150), channel_id=1, source_target_pairs={{0,16},{8,24},{16,0},{24,8},{1,17},{9,25},{17,1},{25,9},{2,18},{10... | collective-permute-start | bytes 331784 | tf_op jit(solution)/shard_map/ppermute | solution.py:31
  (131 shorter events, 72.7 us)
Async XLA Ops:
  4.4 23.7 %copy-start.7 = (f32[1,1,16,24,384]{4,3,2,1,0:T(8,128)}, f32[1,1,16,24,384]{4,3,2,1,0:T(8,128)S(1)}, u32[]{:S(2)}) copy-start(f32[1,1,16,24,384]{4,3,2,1,0:T(8,128)S(1)} %get-tuple-element.38) | copy-start | bytes 1769476
  4.4 23.7 %copy-start.9 = (f32[1,1,16,24,384]{4,3,2,1,0:T(8,128)}, f32[1,1,16,24,384]{4,3,2,1,0:T(8,128)S(1)}, u32[]{:S(2)}) copy-start(f32[1,1,16,24,384]{4,3,2,1,0:T(8,128)S(1)} %get-tuple-element.39) | copy-start | bytes 1769476
  4.5 19.1 %collective-permute-start = (bf16[1,2,16,24,384]{4,3,2,1,0:T(8,128)(2,1)S(1)}, bf16[1,2,16,24,384]{4,3,2,1,0:T(8,128)(2,1)S(1)}, u32[]{:S(2)}, u32[]{:S(2)}) collective-permute-start(bf16[1,2,16,24,384]{4,3,2,1,0:T(8,128)(2,1)S(1)} %pad_maximum_fusion.4), channel_id=1, source_target_pairs={{8,0},{16,8},{24,16},{9,1},{17,9},{25,17},{10,2},{18,10},{26,18},{... | collective-permute-start | bytes 1769480 | tf_op jit(solution)/shard_map/ppermute | solution.py:21
  10.2 23.1 %collective-permute-start.9 = (bf16[1,2,16,24,384]{4,3,2,1,0:T(8,128)(2,1)}, bf16[1,2,16,24,384]{4,3,2,1,0:T(8,128)(2,1)S(1)}, u32[]{:S(2)}, u32[]{:S(2)}) collective-permute-start(bf16[1,2,16,24,384]{4,3,2,1,0:T(8,128)(2,1)} %get-tuple-element.27), channel_id=1, source_target_pairs={{0,8},{8,16},{16,24},{1,9},{9,17},{17,25},{2,10},{10,18},{18,26},{... | collective-permute-start | bytes 1769480 | tf_op jit(solution)/shard_map/ppermute | solution.py:21
  23.7 50.2 %collective-permute-start.2 = (bf16[1,2,16,24,384]{4,3,2,1,0:T(8,128)(2,1)}, bf16[1,2,16,24,384]{4,3,2,1,0:T(8,128)(2,1)}, u32[]{:S(2)}, u32[]{:S(2)}) collective-permute-start(bf16[1,2,16,24,384]{4,3,2,1,0:T(8,128)(2,1)} %get-tuple-element.27), channel_id=1, source_target_pairs={{0,8},{8,0},{16,24},{24,16},{1,9},{9,1},{17,25},{25,17},{2,10},{10... | collective-permute-start | bytes 1769480 | tf_op jit(solution)/shard_map/ppermute | solution.py:171
  26.6 49.3 %collective-permute-start.3 = (bf16[1,2,16,24,384]{4,3,2,1,0:T(8,128)(2,1)}, bf16[1,2,16,24,384]{4,3,2,1,0:T(8,128)(2,1)}, u32[]{:S(2)}, u32[]{:S(2)}) collective-permute-start(bf16[1,2,16,24,384]{4,3,2,1,0:T(8,128)(2,1)} %get-tuple-element.27), channel_id=1, source_target_pairs={{0,16},{8,24},{16,0},{24,8},{1,17},{9,25},{17,1},{25,9},{2,18},{10... | collective-permute-start | bytes 1769480 | tf_op jit(solution)/shard_map/ppermute | solution.py:171
  26.6 54.7 %collective-permute-start.4 = (bf16[1,2,16,24,384]{4,3,2,1,0:T(8,128)(2,1)}, bf16[1,2,16,24,384]{4,3,2,1,0:T(8,128)(2,1)}, u32[]{:S(2)}, u32[]{:S(2)}) collective-permute-start(bf16[1,2,16,24,384]{4,3,2,1,0:T(8,128)(2,1)} %get-tuple-element.27), channel_id=1, source_target_pairs={{0,24},{8,16},{16,8},{24,0},{1,25},{9,17},{17,9},{25,1},{2,26},{10... | collective-permute-start | bytes 1769480 | tf_op jit(solution)/shard_map/ppermute | solution.py:171
  31.3 34.9 %collective-permute-start.5 = (bf16[1,2,16,24,96]{4,3,2,1,0:T(8,128)(2,1)}, bf16[1,2,16,24,96]{4,3,2,1,0:T(8,128)(2,1)}, u32[]{:S(2)}, u32[]{:S(2)}) collective-permute-start(bf16[1,2,16,24,96]{4,3,2,1,0:T(8,128)(2,1)} %get-tuple-element.58), channel_id=1, source_target_pairs={{0,8},{8,0},{16,24},{24,16},{1,9},{9,1},{17,25},{25,17},{2,10},{10... | collective-permute-start | bytes 442376 | tf_op jit(solution)/shard_map/ppermute | solution.py:167
  33.3 35.4 %collective-permute-start.6 = (bf16[1,2,16,24,96]{4,3,2,1,0:T(8,128)(2,1)S(1)}, bf16[1,2,16,24,96]{4,3,2,1,0:T(8,128)(2,1)S(1)}, u32[]{:S(2)}, u32[]{:S(2)}) collective-permute-start(bf16[1,2,16,24,96]{4,3,2,1,0:T(8,128)(2,1)S(1)} %get-tuple-element.57), channel_id=1, source_target_pairs={{0,16},{8,24},{16,0},{24,8},{1,17},{9,25},{17,1},{25,9},{2,18},{10... | collective-permute-start | bytes 442376 | tf_op jit(solution)/shard_map/ppermute | solution.py:167
  66.2 6.6 %collective-permute-start.7 = (bf16[1,2,16,24,96]{4,3,2,1,0:T(8,128)(2,1)S(1)}, bf16[1,2,16,24,96]{4,3,2,1,0:T(8,128)(2,1)S(1)}, u32[]{:S(2)}, u32[]{:S(2)}) collective-permute-start(bf16[1,2,16,24,96]{4,3,2,1,0:T(8,128)(2,1)S(1)} %get-tuple-element.56), channel_id=1, source_target_pairs={{0,24},{8,16},{16,8},{24,0},{1,25},{9,17},{17,9},{25,1},{2,26},{10... | collective-permute-start | bytes 442376 | tf_op jit(solution)/shard_map/ppermute | solution.py:167
  68.7 18.8 %collective-permute-start.10 = (bf16[1,2,16,24,384]{4,3,2,1,0:T(8,128)(2,1)}, bf16[1,2,16,24,384]{4,3,2,1,0:T(8,128)(2,1)}, u32[]{:S(2)}, u32[]{:S(2)}) collective-permute-start(bf16[1,2,16,24,384]{4,3,2,1,0:T(8,128)(2,1)} %fusion.45), channel_id=1, source_target_pairs={{0,8},{8,16},{16,24},{1,9},{9,17},{17,25},{2,10},{10,18},{18,26},{... | collective-permute-start | bytes 1769480 | tf_op jit(solution)/shard_map/ppermute | solution.py:21
  102.8 41.7 %collective-permute-start.11 = (f32[4,144,768]{2,1,0:T(8,128)}, f32[4,144,768]{2,1,0:T(8,128)}, u32[]{:S(2)}, u32[]{:S(2)}) collective-permute-start(f32[4,144,768]{2,1,0:T(8,128)} %dynamic-slice_bitcast_fusion), channel_id=1, source_target_pairs={{0,1},{1,0},{2,3},{3,2},{4,5},{5,4},{6,7},{7,6},{8,9},{9,8},{10,11... | collective-permute-start | bytes 5308424 | tf_op jit(solution)/shard_map/ppermute | solution.py:43
  122.7 24.8 %collective-permute-start.8 = (f32[4,1296,96]{1,2,0:T(8,128)}, f32[4,1296,96]{1,2,0:T(8,128)}, u32[]{:S(2)}, u32[]{:S(2)}) collective-permute-start(f32[4,1296,96]{1,2,0:T(8,128)} %bitcast.146), channel_id=1, source_target_pairs={{0,1},{1,0},{2,3},{3,2},{4,5},{5,4},{6,7},{7,6},{8,9},{9,8},{10,11... | collective-permute-start | bytes 5971976 | tf_op jit(solution)/shard_map/ppermute | solution.py:43
  123.2 19.8 %collective-permute-start.1 = (bf16[1,2,16,24,384]{4,3,2,1,0:T(8,128)(2,1)}, bf16[1,2,16,24,384]{4,3,2,1,0:T(8,128)(2,1)}, u32[]{:S(2)}, u32[]{:S(2)}) collective-permute-start(bf16[1,2,16,24,384]{4,3,2,1,0:T(8,128)(2,1)} %fusion.54), channel_id=1, source_target_pairs={{8,0},{16,8},{24,16},{9,1},{17,9},{25,17},{10,2},{18,10},{26,18},{... | collective-permute-start | bytes 1769480 | tf_op jit(solution)/shard_map/ppermute | solution.py:21
  124.8 19.6 %copy-start.5 = (f32[1152,768]{1,0:T(8,128)S(1)}, f32[1152,768]{1,0:T(8,128)}, u32[]{:S(2)}) copy-start(f32[1152,768]{1,0:T(8,128)} %copy.34) | copy-start | bytes 10616836
  178.5 51.6 %collective-permute-start.14 = (bf16[1296,96]{0,1:T(8,128)(2,1)}, bf16[1296,96]{0,1:T(8,128)(2,1)}, u32[]{:S(2)}, u32[]{:S(2)}) collective-permute-start(bf16[1296,96]{0,1:T(8,128)(2,1)} %get-tuple-element.42), channel_id=1, source_target_pairs={{0,6},{1,7},{2,4},{3,5},{4,2},{5,3},{6,0},{7,1},{8,14},{9,15},{10,... | collective-permute-start | bytes 746504 | tf_op jit(solution)/shard_map/ppermute | solution.py:54
  182.2 48.1 %collective-permute-start.13 = (bf16[1296,96]{0,1:T(8,128)(2,1)}, bf16[1296,96]{0,1:T(8,128)(2,1)}, u32[]{:S(2)}, u32[]{:S(2)}) collective-permute-start(bf16[1296,96]{0,1:T(8,128)(2,1)} %get-tuple-element.43), channel_id=1, source_target_pairs={{0,4},{1,5},{2,6},{3,7},{4,0},{5,1},{6,2},{7,3},{8,12},{9,13},{10,... | collective-permute-start | bytes 746504 | tf_op jit(solution)/shard_map/ppermute | solution.py:54
  183.5 17.0 %collective-permute-start.17 = (bf16[144,768]{1,0:T(8,128)(2,1)S(1)}, bf16[144,768]{1,0:T(8,128)(2,1)S(1)}, u32[]{:S(2)}, u32[]{:S(2)}) collective-permute-start(bf16[144,768]{1,0:T(8,128)(2,1)S(1)} %get-tuple-element.45), channel_id=1, source_target_pairs={{0,6},{1,7},{2,4},{3,5},{4,2},{5,3},{6,0},{7,1},{8,14},{9,15},{10,... | collective-permute-start | bytes 663560 | tf_op jit(solution)/shard_map/ppermute | solution.py:54
  185.5 38.6 %collective-permute-start.16 = (bf16[144,768]{1,0:T(8,128)(2,1)S(1)}, bf16[144,768]{1,0:T(8,128)(2,1)S(1)}, u32[]{:S(2)}, u32[]{:S(2)}) collective-permute-start(bf16[144,768]{1,0:T(8,128)(2,1)S(1)} %get-tuple-element.46), channel_id=1, source_target_pairs={{0,4},{1,5},{2,6},{3,7},{4,0},{5,1},{6,2},{7,3},{8,12},{9,13},{10,... | collective-permute-start | bytes 663560 | tf_op jit(solution)/shard_map/ppermute | solution.py:54
  186.6 37.5 %collective-permute-start.15 = (bf16[144,768]{1,0:T(8,128)(2,1)S(1)}, bf16[144,768]{1,0:T(8,128)(2,1)S(1)}, u32[]{:S(2)}, u32[]{:S(2)}) collective-permute-start(bf16[144,768]{1,0:T(8,128)(2,1)S(1)} %get-tuple-element.44), channel_id=1, source_target_pairs={{0,2},{1,3},{2,0},{3,1},{4,6},{5,7},{6,4},{7,5},{8,10},{9,11},{10,... | collective-permute-start | bytes 663560 | tf_op jit(solution)/shard_map/ppermute | solution.py:54
  200.5 29.7 %collective-permute-start.12 = (bf16[1296,96]{0,1:T(8,128)(2,1)}, bf16[1296,96]{0,1:T(8,128)(2,1)S(1)}, u32[]{:S(2)}, u32[]{:S(2)}) collective-permute-start(bf16[1296,96]{0,1:T(8,128)(2,1)} %get-tuple-element.41), channel_id=1, source_target_pairs={{0,2},{1,3},{2,0},{3,1},{4,6},{5,7},{6,4},{7,5},{8,10},{9,11},{10,... | collective-permute-start | bytes 746504 | tf_op jit(solution)/shard_map/ppermute | solution.py:54
  226.2 7.4 %collective-permute-start.20 = (f32[144,192]{1,0:T(8,128)S(1)}, f32[144,192]{1,0:T(8,128)S(1)}, u32[]{:S(2)}, u32[]{:S(2)}) collective-permute-start(f32[144,192]{1,0:T(8,128)S(1)} %bitcast.149), channel_id=1, source_target_pairs={{0,24},{8,16},{16,8},{24,0},{1,25},{9,17},{17,9},{25,1},{2,26},{10... | collective-permute-start | bytes 331784 | tf_op jit(solution)/shard_map/ppermute | solution.py:31
  226.3 8.8 %collective-permute-start.19 = (f32[144,192]{1,0:T(8,128)S(1)}, f32[144,192]{1,0:T(8,128)S(1)}, u32[]{:S(2)}, u32[]{:S(2)}) collective-permute-start(f32[144,192]{1,0:T(8,128)S(1)} %bitcast.150), channel_id=1, source_target_pairs={{0,16},{8,24},{16,0},{24,8},{1,17},{9,25},{17,1},{25,9},{2,18},{10... | collective-permute-start | bytes 331784 | tf_op jit(solution)/shard_map/ppermute | solution.py:31
  230.1 5.2 %collective-permute-start.18 = (f32[144,192]{1,0:T(8,128)S(1)}, f32[144,192]{1,0:T(8,128)S(1)}, u32[]{:S(2)}, u32[]{:S(2)}) collective-permute-start(f32[144,192]{1,0:T(8,128)S(1)} %bitcast.151), channel_id=1, source_target_pairs={{0,8},{8,0},{16,24},{24,16},{1,9},{9,1},{17,25},{25,17},{2,10},{10... | collective-permute-start | bytes 331784 | tf_op jit(solution)/shard_map/ppermute | solution.py:31
  (12 other events, 87.9 us)
